TPU v7x, 512 devices: a whole 4x8x8 slice. The times are simulated.
512 devices in a mesh: blk: 64 (over z_hi, x, y), rd: 8 (over z_lo, core).
Axes of the slice: x: 4, y: 8, z: 8 (z_hi: 2, z_lo: 4; z = z_hi * 4 + z_lo), core: 2. Of those that a mesh axis runs over, the one named last changes fastest.
Arguments:
- factor: float32 [18432, 8, 2304], P('blk', 'rd'), as said below
- panel: float32 [18432, 1024], P(('blk', 'rd')), may hold values from -6 to 6
Outputs:
- new_panel: float32 [18432, 1024], P('blk')
- values: float32 [1024], replicated
Inputs may be any that keep to these rules, and one draw needn't show every extreme that they name: L built from factor is symmetric and positive definite.
All inputs are finite; a program needn't handle non-finite values.
Results may differ from a plain program's by a relative error of at most 0.000073.
Values sent between devices are 32-bit elements; how exact they have to be, the bound alone decides.
A program may use at most 128 MiB of HBM per device.

v0:
```python
import jax
import jax.numpy as jnp
from jax import lax
from jax.sharding import PartitionSpec as P

N = 18432


def inner_cols(left, right):
    return lax.dot_general(
        left,
        right,
        (((0,), (0,)), ((), ())),
        precision=lax.Precision.HIGHEST,
        preferred_element_type=jnp.float32,
    )


def body(factor, panel):
    rows = factor.shape[0]
    width = panel.shape[1]
    local = factor.reshape(rows, -1)
    partial_value = jnp.dot(
        local,
        lax.all_gather(panel, "blk", axis=0, tiled=True),
        precision=lax.Precision.HIGHEST,
        preferred_element_type=jnp.float32,
    )
    image = lax.psum_scatter(partial_value, "rd", scatter_dimension=0, tiled=True)
    halfway = width // 2
    left_cols = image[:, :halfway]
    right_cols = image[:, halfway:]
    upper_left, upper_right, lower_right = lax.psum(
        (
            inner_cols(left_cols, left_cols),
            inner_cols(left_cols, right_cols),
            inner_cols(right_cols, right_cols),
        ),
        ("blk", "rd"),
    )
    top_rows = jnp.concatenate([upper_left, upper_right], axis=1)
    low_rows = jnp.concatenate([upper_right.T, lower_right], axis=1)
    gram = jnp.concatenate([top_rows, low_rows], axis=0) / N
    lower = jnp.linalg.cholesky(gram)
    basis = jax.scipy.linalg.solve_triangular(lower, image.T, lower=True).T
    new_panel = lax.all_gather(basis, "rd", axis=0, tiled=True)
    numer, squares = lax.psum(
        (jnp.sum(panel * image, axis=0), jnp.sum(panel * panel, axis=0)), ("blk", "rd")
    )
    values = numer / N / (squares / N + 1e-06)
    return (new_panel, values)


def solution(mesh):
    placed = (P("blk", "rd", None), P(("blk", "rd"), None))
    return jax.shard_map(
        body, mesh=mesh, in_specs=placed, out_specs=(P("blk", None), P()), check_vma=False
    )
```

profile of v0, /device:TPU:1, one launch (start us, length us, event | category | flops | bytes accessed | tf_op | source)
XLA Modules:
  0.0 1085.5 jit_solution(3195490097116594538)
XLA Ops:
  8.0 233.5 %all-gather.5.cloned.1.call-done = f32[64,36,1024]{2,1,0:T(8,128)} async-done(((f32[1,36,1024]{2,1,0:T(8,128)}), f32[64,36,1024]{2,1,0:T(8,128)}) %all-gather.5.cloned.1.call-update) | async-done | bytes 9437200 | tf_op jit(solution)/shard_map/all_gather | solution.py:25
  241.5 9.9 reshape.107
  251.4 12.3 %fusion.1 = f32[288,1024]{1,0:T(8,128)} fusion(f32[2304,1024]{1,0:T(8,128)} %reshape.107, f32[288,1,2304]{2,1,0:T(1,128)S(1)} %copy-done.2), kind=kOutput, calls=%fused_computation.7 | convolution fusion | flops 8153726976 | bytes 13271040 | tf_op jit(solution)/shard_map/dot_general | solution.py:23
  265.7 71.9 %all-reduce.7.cloned.1.call-done = f32[288,1024]{1,0:T(8,128)} async-done(((f32[288,1024]{1,0:T(8,128)}), f32[288,1024]{1,0:T(8,128)}) %all-reduce.7.cloned.1.call-update) | async-done | bytes 1179664
  347.8 282.9 %all-reduce.9.cloned.1.call-done = (f32[512,512]{0,1:T(8,128)}, f32[512,512]{1,0:T(8,128)}, f32[512,512]{1,0:T(8,128)}) async-done(((f32[512,512]{0,1:T(8,128)}, f32[512,512]{1,0:T(8,128)}, f32[512,512]{1,0:T(8,128)}), (f32[512,512]{0,1:T(8,128)}, f32[512,512]{1,0:T(8,128)}, f32[512,512]{1,0:T(8,128)})) %all-reduce.9.cloned.1.call-update) | async-done | bytes 3145744 | tf_op jit(solution)/shard_map/psum | solution.py:33
  639.8 5.8 copy.12
  651.0 11.7 %cholesky.223 = f32[128,128]{1,0:T(8,128)S(1)} custom-call(f32[128,128]{1,0:T(8,128)S(1)} %cholesky.580), custom_call_target="Cholesky" | custom-call | tf_op jit(solution)/shard_map/jit(cholesky)/cholesky | solution.py:44
  665.3 9.8 custom-call.63
  679.1 11.9 %cholesky.244 = f32[128,128]{1,0:T(8,128)S(1)} custom-call(f32[128,128]{1,0:T(8,128)S(1)} %cholesky.584), custom_call_target="Cholesky" | custom-call | tf_op jit(solution)/shard_map/jit(cholesky)/cholesky | solution.py:44
  691.6 9.8 custom-call.64
  704.7 11.7 %cholesky.468 = f32[128,128]{1,0:T(8,128)S(1)} custom-call(f32[128,128]{1,0:T(8,128)S(1)} %cholesky.589), custom_call_target="Cholesky" | custom-call | tf_op jit(solution)/shard_map/jit(cholesky)/cholesky | solution.py:44
  717.7 9.8 custom-call.65
  731.0 11.9 %cholesky.487 = f32[128,128]{1,0:T(8,128)S(1)} custom-call(f32[128,128]{1,0:T(8,128)S(1)} %cholesky.594), custom_call_target="Cholesky" | custom-call | tf_op jit(solution)/shard_map/jit(cholesky)/cholesky | solution.py:44
  744.2 9.8 custom-call.66
  757.5 11.7 %cholesky.506 = f32[128,128]{1,0:T(8,128)S(1)} custom-call(f32[128,128]{1,0:T(8,128)S(1)} %cholesky.599), custom_call_target="Cholesky" | custom-call | tf_op jit(solution)/shard_map/jit(cholesky)/cholesky | solution.py:44
  770.5 10.2 custom-call.67
  784.0 11.7 %cholesky.526 = f32[128,128]{1,0:T(8,128)S(1)} custom-call(f32[128,128]{1,0:T(8,128)S(1)} %cholesky.604), custom_call_target="Cholesky" | custom-call | tf_op jit(solution)/shard_map/jit(cholesky)/cholesky | solution.py:44
  797.0 9.8 custom-call.68
  809.8 11.9 %cholesky.546 = f32[128,128]{1,0:T(8,128)S(1)} custom-call(f32[128,128]{1,0:T(8,128)S(1)} %cholesky.609), custom_call_target="Cholesky" | custom-call | tf_op jit(solution)/shard_map/jit(cholesky)/cholesky | solution.py:44
  822.9 9.8 custom-call.69
  835.4 11.7 %cholesky.564 = f32[128,128]{1,0:T(8,128)S(1)} custom-call(f32[128,128]{1,0:T(8,128)S(1)} %convolution_subtract_fusion.6), custom_call_target="Cholesky" | custom-call | tf_op jit(solution)/shard_map/jit(cholesky)/cholesky | solution.py:44
  858.8 27.8 %while.1 = (s32[]{:T(128)}, f32[1024,1024]{1,0:T(8,128)}, s32[8,2]{0,1:T(2,128)S(1)}, f32[8,128,128]{2,1,0:T(8,128)}, s32[]{:T(128)}) while((s32[]{:T(128)}, f32[1024,1024]{1,0:T(8,128)}, s32[8,2]{0,1:T(2,128)S(1)}, f32[8,128,128]{2,1,0:T(8,128)}, s32[]{:T(128)}) %tuple.63), condition=%wide.while_cond, body=%wide.while_body.sunk | while | flops 2 | bytes 132705 | solution.py:45
  886.6 79.6 %custom-call.70 = f32[8,128,128]{1,2,0:T(8,128)S(1)} custom-call(f32[8,128,128]{2,1,0:T(8,128)} %get-tuple-element.9), custom_call_target="InvertDiagBlocksLowerTriangular" | custom-call | tf_op jit(solution)/shard_map/jit(_solve_triangular)/triangular_solve | solution.py:45
  978.0 97.7 %all-reduce.2 = (f32[1024]{0:T(1024)S(1)}, f32[1024]{0:T(1024)S(1)}) all-reduce(f32[1024]{0:T(1024)S(1)} %get-tuple-element.11, f32[1024]{0:T(1024)S(1)} %get-tuple-element.10), channel_id=1, replica_groups=mesh['blk'=64,'rd'=8] {'blk','rd'}, use_global_device_ids=true, to_apply=%region_23.24 | all-reduce | flops 2048 | bytes 16384 | tf_op jit(solution)/shard_map/psum | solution.py:47
  (110 shorter events, 108.7 us)
Async XLA Ops:
  7.2 234.3 %all-gather.5.cloned.1.call-start = ((), (), s32[]{:S(2)}) async-start(), calls=%async_computation | async-start | bytes 10649600 | tf_op jit(solution)/shard_map/all_gather | solution.py:25
  7.9 243.5 %copy-start.2 = (f32[288,1,2304]{2,1,0:T(1,128)S(1)}, f32[288,1,2304]{2,1,0:T(1,128)}, u32[]{:S(2)}) copy-start(f32[288,1,2304]{2,1,0:T(1,128)} %param.2) | copy-start | bytes 7962628
  7.9 329.7 %all-reduce.7.cloned.1.call-start = ((), (), s32[]{:S(2)}) async-start(), calls=%async_computation.2 | async-start | bytes 2359296
  263.7 83.1 %copy-start.3 = (f32[36,1024]{1,0:T(8,128)S(1)}, f32[36,1024]{1,0:T(8,128)}, u32[]{:S(2)}) copy-start(f32[36,1024]{1,0:T(8,128)} %param.3) | copy-start | bytes 442372
  263.7 367.0 %all-reduce.9.cloned.1.call-start = ((), (), s32[]{:S(2)}) async-start(), calls=%async_computation.3 | async-start | bytes 6291456 | tf_op jit(solution)/shard_map/psum | solution.py:33
  346.7 729.6 %all-gather.7.cloned.1.call-start = ((), (), s32[]{:S(2)}) async-start(), calls=%async_computation.1 | async-start | bytes 1474560 | tf_op jit(solution)/shard_map/all_gather | solution.py:46
  630.7 5.1 copy-start.1
  649.1 1.9 copy-start
  977.3 0.7 copy-start.4
Sparse Core Ops, SparseCore 0:
  12.5 228.9 all-gather.4
  263.9 73.6 all-reduce.6
  346.9 283.8 all-reduce.8
  978.1 35.1 all-gather.6
where the time goes:
time: 1090 us
  waiting for transfers between devices  589 us (54%)
  other arithmetic  269 us (25%)
  blocking collectives  97.7 us (9%)
  matrix products  55.5 us (5%)
  local copies, waits for them, and re-layouts  54.3 us (5%)
  between operations  19.9 us (2%)
    psum x1, waiting for transfers between devices, body(): lax.psum((inner_cols(left_cols, left_cols), inner_cols(left_cols, right_c...  283 us
    all_gather x1, waiting for transfers between devices, body(): lax.all_gather(panel, 'blk', axis=0, tiled=True)  234 us
    another operation x30, other arithmetic, body(): lower = jnp.linalg.cholesky(gram)  172 us
    psum x1, blocking collectives, body(): lax.psum((jnp.sum(panel * image, axis=0), jnp.sum(panel * panel, axis=0))...  97.7 us
    another operation x3, other arithmetic, body(): basis = jax.scipy.linalg.solve_triangular(lower, image.T, lower=True).T  84.4 us
    unnamed x5, waiting for transfers between devices  72.6 us
    another operation x24, local copies, waits for them, and re-layouts  27.8 us
    another operation x14, matrix products, body(): lower = jnp.linalg.cholesky(gram)  23.1 us
  transfers between devices with their start and end apart: 4, of which 3 were waited for; matrix products, arithmetic and copies ran while one was open for 0% of the time, Pallas kernels for 0%

commit v1 on v0

v1 whole, which is shorter than its diff:
```python
import heapq

import jax
import jax.numpy as jnp
from jax import lax
from jax.experimental import pallas as pl
from jax.experimental.pallas import tpu as pltpu
from jax.sharding import PartitionSpec as P

N = 18432
X, Y, Z = 4, 8, 4
ROWS = 36
SHARD = ROWS * 8
BLOCK = 288
CHUNK = 80
SLICE = 8 * CHUNK
MESH = pl.DeviceIdType.MESH
HIGHEST = lax.Precision.HIGHEST


def nt(a, b):
    return lax.dot_general(
        a,
        b,
        (((1,), (1,)), ((), ())),
        precision=HIGHEST,
        preferred_element_type=jnp.float32,
    )


def ring(n):
    h = n // 2
    for sign in (1, -1):
        for t in range(h - 1):
            yield sign, sign * t, None
        yield sign, sign * (h - 1), 0 if sign > 0 else 1


def order(messages, preset=()):
    waiting = {k: set(m[3]) - set(preset) for k, m in messages.items()}
    followers = {}
    for k, m in messages.items():
        for d in m[3]:
            followers.setdefault(d, []).append(k)
    free, heap, events = {}, [], []

    def start(k, now):
        link, size, latency, _ = messages[k]
        begin = max(now, free.get(link, 0.0))
        free[link] = begin + size
        events.append(("start", k))
        heapq.heappush(heap, (begin + size + latency, len(events), k))

    for k in messages:
        if not waiting[k]:
            start(k, 0.0)
    while heap:
        now, _, k = heapq.heappop(heap)
        events.append(("wait", k))
        for f in followers.get(k, ()):
            waiting[f].discard(k)
            if not waiting[f]:
                start(f, now)
    assert sum(e == "start" for e, _ in events) == len(messages)
    return events


def panel_messages():
    rate = 50e3
    out = {}
    meta = {}
    z_key = ("z",)
    out[z_key] = ("z", SHARD * 512 / 25e3, 3.0, ())
    meta[z_key] = ("z", 0, 0, 0, 0, SHARD)
    for z in range(2):
        base = (z_key,) if z else ()
        for part, (first, rows) in enumerate(((0, 22), (22, 14))):
            axes = (("y", Y), ("x", X)) if part == 0 else (("x", X), ("y", Y))
            (f_name, f_n), (s_name, s_n) = axes
            half = rows // 2

            def cut(piece):
                return (first, rows) if piece is None else (first + piece * half, half)

            def offset(f, s):
                return (f, s) if f_name == "x" else (s, f)

            delivered = {0: base}
            for sign, at, piece in ring(f_n):
                key = (z, part, "f", 0, sign, at)
                dep = base if at == 0 else ((z, part, "f", 0, sign, at - sign),)
                start, count = cut(piece)
                ox, oy = offset(at, 0)
                out[key] = (f_name + str(sign), count * 4096 / rate, 1.0, dep)
                meta[key] = (f_name, sign, z, ox, oy, start * 8, count * 8)
                to = (at + sign) % f_n
                delivered[to] = delivered.get(to, ()) + (key,)
            for f in sorted(delivered, key=lambda v: min(v, f_n - v)):
                for sign, at, piece in ring(s_n):
                    key = (z, part, "s", f, sign, at)
                    dep = delivered[f] if at == 0 else ((z, part, "s", f, sign, at - sign),)
                    start, count = cut(piece)
                    ox, oy = offset(f, at)
                    out[key] = (s_name + str(sign), count * 4096 / rate, 1.0, dep)
                    meta[key] = (s_name, sign, z, ox, oy, start * 8, count * 8)
    return out, meta


def gram_messages():
    out = {}
    meta = {}
    delivered = {0: ()}
    for sign, at, piece in ring(Y):
        key = ("y", sign, at)
        dep = () if at == 0 else (("y", sign, at - sign),)
        first, count = (0, Z) if piece is None else (piece * Z // 2, Z // 2)
        out[key] = ("y" + str(sign), count * CHUNK * 512 / 50e3, 1.0, dep)
        meta[key] = ("y", sign, at, first, count)
        to = (at + sign) % Y
        delivered[to] = delivered.get(to, ()) + (key,)
    for f, dep in delivered.items():
        key = ("core", f)
        out[key] = ("core", Z * CHUNK * 512 / 400e3, 0.5, dep)
        meta[key] = ("core", 0, f, 0, Z)
    return out, meta


PANEL_MESSAGES, PANEL_META = panel_messages()
PANEL_EVENTS = order(PANEL_MESSAGES)
PANEL_SLOT = {k: i for i, k in enumerate(PANEL_MESSAGES)}
GRAM_MESSAGES, GRAM_META = gram_messages()
GRAM_EVENTS = order(GRAM_MESSAGES)
GRAM_SLOT = {k: i for i, k in enumerate(GRAM_MESSAGES)}


def combine_kernel(
    factor_ref,
    panel_ref,
    image_ref,
    parts_ref,
    gathered,
    high,
    low,
    partial,
    from_core,
    from_z,
    local,
    from_y,
    total_y,
    from_x,
    total_x,
    from_hi,
    p_send,
    p_recv,
    r_send,
    r_recv,
    a_send,
    a_recv,
    y_send,
    y_recv,
    x_send,
    x_recv,
    h_send,
    h_recv,
    c_send,
    c_recv,
    g_send,
    g_recv,
):
    blk = lax.axis_index("blk")
    rd = lax.axis_index("rd")
    hi, x, y = blk // (X * Y), (blk // Y) % X, blk % Y
    z, core = rd // 2, rd % 2

    def at_blk(h, i, j):
        return (h * X + i) * Y + j

    def wrap(v, n):
        return lax.rem(v + n, n)

    def x_peer(d):
        return (at_blk(hi, wrap(x + d, X), y), rd)

    def y_peer(d):
        return (at_blk(hi, x, wrap(y + d, Y)), rd)

    def z_peer(d):
        return (blk, wrap(z + d, Z) * 2 + core)

    hi_peer = (at_blk(1 - hi, x, y), rd)
    core_peer = (blk, z * 2 + 1 - core)

    def remote(src, dst, send, recv, peer):
        return pltpu.make_async_remote_copy(
            src_ref=src,
            dst_ref=dst,
            send_sem=send,
            recv_sem=recv,
            device_id=peer,
            device_id_type=MESH,
        )

    barrier = pltpu.get_barrier_semaphore()
    peers = [x_peer(d) for d in range(1, X)] + [y_peer(d) for d in range(1, Y)]
    peers += [z_peer(d) for d in range(1, Z)] + [hi_peer, core_peer]
    for peer in peers:
        pl.semaphore_signal(barrier, inc=1, device_id=peer, device_id_type=MESH)

    own = pl.multiple_of(blk * SHARD, 8)
    gathered[pl.ds(own, SHARD), :] = panel_ref[...]
    pl.semaphore_wait(barrier, len(peers))

    def panel_copy(key, arrived):
        axis, sign, far, ox, oy, *span = PANEL_META[key]
        slot = PANEL_SLOT[key]
        if axis == "z":
            peer = hi_peer
            source = 1 - hi if arrived else hi
            start, count = 0, SHARD
            origin = at_blk(source, x, y)
        else:
            peer = x_peer(sign) if axis == "x" else y_peer(sign)
            start, count = span
            if arrived:
                ox, oy = (ox + sign, oy) if axis == "x" else (ox, oy + sign)
            source = 1 - hi if far else hi
            origin = at_blk(source, wrap(x - ox % X, X), wrap(y - oy % Y, Y))
        where = pl.ds(pl.multiple_of(origin * SHARD + start, 8), count)
        return remote(
            gathered.at[where], gathered.at[where], p_send.at[slot], p_recv.at[slot], peer
        )

    started = 0
    for event, key in PANEL_EVENTS:
        if event == "start":
            panel_copy(key, False).start()
        else:
            if started == 0:
                started = 1

                def split(i, carry):
                    rows = pl.ds(pl.multiple_of(i * 16, 16), 16)
                    value = factor_ref[rows, :]
                    top = value.astype(jnp.bfloat16)
                    high[rows, :] = top
                    low[rows, :] = (value - top.astype(jnp.float32)).astype(jnp.bfloat16)
                    return carry

                lax.fori_loop(0, BLOCK // 16, split, 0)
            panel_copy(key, True).wait_recv()
    for key in PANEL_MESSAGES:
        panel_copy(key, False).wait_send()

    for q in range(4):
        right = jnp.concatenate(
            [gathered[pl.ds(2 * q + s, 8 * BLOCK, stride=8), :] for s in range(2)], axis=1
        )
        r_top = right.astype(jnp.bfloat16)
        r_low = (right - r_top.astype(jnp.float32)).astype(jnp.bfloat16)
        product = (
            jnp.dot(low[...], r_top, preferred_element_type=jnp.float32)
            + jnp.dot(high[...], r_low, preferred_element_type=jnp.float32)
            + jnp.dot(high[...], r_top, preferred_element_type=jnp.float32)
        )
        partial[q, 0] = product[:, :128]
        partial[q, 1] = product[:, 128:]

    to_core = remote(
        partial.at[:, 1 - core], from_core, r_send.at[0], r_recv.at[0], core_peer
    )
    to_core.start()
    to_core.wait()
    for k in range(Z):
        from_core[k] += partial[k, core]
    to_z = [
        remote(
            from_core.at[wrap(z + d, Z)],
            from_z.at[d - 1],
            r_send.at[d],
            r_recv.at[d],
            z_peer(d),
        )
        for d in range(1, Z)
    ]
    for copy in to_z:
        copy.start()
    for copy in to_z:
        copy.wait()
    image_ref[z, core] = from_core[z] + from_z[0] + from_z[1] + from_z[2]

    def spread(d, arrived):
        who = wrap(z - d, Z) if arrived else z
        where = image_ref.at[who, core]
        return remote(where, where, a_send.at[d], a_recv.at[d], z_peer(d))

    def share(k, arrived):
        who = wrap(z - k, Z)
        where = image_ref.at[who, 1 - core if arrived else core]
        return remote(where, where, a_send.at[Z + k], a_recv.at[Z + k], core_peer)

    for d in range(1, Z):
        spread(d, False).start()
    share(0, False).start()
    for d in range(1, Z):
        spread(d, True).wait_recv()
        share(d, False).start()
    for d in range(Z):
        share(d, True).wait_recv()
    for d in range(1, Z):
        spread(d, False).wait_send()
    for d in range(Z):
        share(d, False).wait_send()

    def group(g):
        return image_ref[g // 2, g % 2]

    mine = group(rd).T
    for d in range(4):
        local[d * 128 : d * 128 + 128, :] = jnp.dot(
            mine, group(wrap(rd + d, 8)), precision=HIGHEST, preferred_element_type=jnp.float32
        )
    lower_half = rd % 4
    local[512:640, :] = jnp.dot(
        group(lower_half).T,
        group(lower_half + 4),
        precision=HIGHEST,
        preferred_element_type=jnp.float32,
    )

    @pl.when(rd >= 4)
    def _():
        local[512:576, :] = local[576:640, :]

    def sums(i, carry):
        numer, squares = carry
        old = panel_ref[pl.ds(pl.multiple_of(i * 8, 8), 8), :]
        new = jnp.concatenate(
            [image_ref[g // 2, g % 2, pl.ds(rd * ROWS + i, 1), :] for g in range(8)], axis=0
        )
        return numer + old * new, squares + old * old

    zero = jnp.zeros((8, 128), jnp.float32)
    numer, squares = lax.fori_loop(0, ROWS, sums, (zero, zero))
    local[576:584, :] = numer
    local[584:592, :] = squares
    local[592:640, :] = jnp.zeros((48, 128), jnp.float32)

    def to_y(d):
        where = pl.ds(pl.multiple_of(wrap(y + d, Y) * CHUNK, 8), CHUNK)
        return remote(
            local.at[where], from_y.at[d - 1], y_send.at[d - 1], y_recv.at[d - 1], y_peer(d)
        )

    for d in range(1, Y):
        to_y(d).start()
    for d in range(1, Y):
        to_y(d).wait()
    chunk = local[pl.ds(pl.multiple_of(y * CHUNK, 8), CHUNK), :]
    for d in range(Y - 1):
        chunk = chunk + from_y[d]
    total_y[...] = chunk
    from_x[x] = chunk

    def to_x(d, arrived):
        slot = wrap(x - d, X) if arrived else x
        return remote(
            total_y, from_x.at[slot], x_send.at[d - 1], x_recv.at[d - 1], x_peer(d)
        )

    for d in range(1, X):
        to_x(d, False).start()
    for d in range(1, X):
        to_x(d, True).wait_recv()
    for d in range(1, X):
        to_x(d, False).wait_send()
    total_x[...] = (from_x[0] + from_x[1]) + (from_x[2] + from_x[3])
    to_hi = remote(total_x, from_hi, h_send.at[0], h_recv.at[0], hi_peer)
    to_hi.start()
    to_hi.wait()
    here = pl.ds(pl.multiple_of(y * CHUNK, 8), CHUNK)
    parts_ref[z, core, here, :] = (total_x[...] + from_hi[...]) * (1.0 / N)

    def chunk_z(d, arrived):
        who = wrap(z - d, Z) if arrived else z
        where = parts_ref.at[who, core, here]
        return remote(where, where, c_send.at[d - 1], c_recv.at[d - 1], z_peer(d))

    for d in range(1, Z):
        chunk_z(d, False).start()
    for d in range(1, Z):
        chunk_z(d, True).wait_recv()
    for d in range(1, Z):
        chunk_z(d, False).wait_send()

    def gram_copy(key, arrived):
        kind, sign, at, first, count = GRAM_META[key]
        slot = GRAM_SLOT[key]
        side = core
        peer = core_peer
        if kind == "y":
            peer = y_peer(sign)
            at = at + sign if arrived else at
        elif arrived:
            side = 1 - core
        rows = pl.ds(pl.multiple_of(wrap(y - at % Y, Y) * CHUNK, 8), CHUNK)
        where = parts_ref.at[pl.ds(first, count), side, rows]
        return remote(where, where, g_send.at[slot], g_recv.at[slot], peer)

    for event, key in GRAM_EVENTS:
        if event == "start":
            gram_copy(key, False).start()
        else:
            gram_copy(key, True).wait_recv()
    for key in GRAM_MESSAGES:
        gram_copy(key, False).wait_send()


def combine(factor, panel):
    f32, bf16 = jnp.float32, jnp.bfloat16
    vmem = pl.BlockSpec(memory_space=pltpu.VMEM)

    def pair(n):
        return [pltpu.SemaphoreType.DMA((n,)), pltpu.SemaphoreType.DMA((n,))]

    return pl.pallas_call(
        combine_kernel,
        out_shape=(
            jax.ShapeDtypeStruct((Z, 2, BLOCK, 128), f32),
            jax.ShapeDtypeStruct((Z, 2, SLICE, 128), f32),
        ),
        in_specs=[vmem, vmem],
        out_specs=(vmem, vmem),
        scratch_shapes=[
            pltpu.VMEM((64 * SHARD, 128), f32),
            pltpu.VMEM((BLOCK, 8 * BLOCK), bf16),
            pltpu.VMEM((BLOCK, 8 * BLOCK), bf16),
            pltpu.VMEM((Z, 2, BLOCK, 128), f32),
            pltpu.VMEM((Z, BLOCK, 128), f32),
            pltpu.VMEM((Z - 1, BLOCK, 128), f32),
            pltpu.VMEM((SLICE, 128), f32),
            pltpu.VMEM((Y - 1, CHUNK, 128), f32),
            pltpu.VMEM((CHUNK, 128), f32),
            pltpu.VMEM((X, CHUNK, 128), f32),
            pltpu.VMEM((CHUNK, 128), f32),
            pltpu.VMEM((CHUNK, 128), f32),
            *pair(len(PANEL_MESSAGES)),
            *pair(Z),
            *pair(2 * Z),
            *pair(Y - 1),
            *pair(X - 1),
            *pair(1),
            *pair(Z - 1),
            *pair(len(GRAM_MESSAGES)),
        ],
        compiler_params=pltpu.CompilerParams(
            collective_id=0, has_side_effects=True, vmem_limit_bytes=50 << 20
        ),
        cost_estimate=pl.CostEstimate(
            flops=5 * 10**9, bytes_accessed=8 << 20, transcendentals=0
        ),
        name="combine",
    )(factor, panel)


def invert_block(a, out_ref):
    sub = lax.broadcasted_iota(jnp.int32, (8, 128), 0)
    lane = lax.broadcasted_iota(jnp.int32, (8, 128), 1)
    left = [a[8 * g:8 * g + 8, :] for g in range(16)]
    right = [jnp.where(lane == sub + 8 * g, 1.0, 0.0) for g in range(16)]
    def column(tile, at):
        return jnp.broadcast_to(tile[:, at:at + 1], (8, 128))
    def row(tile, at):
        return jnp.broadcast_to(tile[at:at + 1, :], (8, 128))
    for p in range(16):
        at, eye = left[p], right[p]
        cols = [column(at, 8 * p + k) for k in range(8)]
        heads, recips, pivots, marks = {}, [], [], []
        for k in range(8):
            d = row(cols[k], k)
            r = 1.0 / d
            m = jnp.where(sub > k, cols[k] * r, 0.0)
            u, w = row(at, k), row(eye, k)
            out_ref[8 * p + k:8 * p + k + 1, :] = (w * lax.rsqrt(d))[0:1, :]
            for c in range(k + 1, 8):
                heads[k, c] = row(cols[c], k)
                cols[c] = cols[c] - m * heads[k, c]
            at = at - m * u
            eye = eye - m * w
            recips.append(r); pivots.append(u); marks.append(w)
        for g in range(p + 1, 16):
            c_g = [column(left[g], 8 * p + k) for k in range(8)]
            lg, rg = left[g], right[g]
            for k in range(8):
                m = c_g[k] * recips[k]
                for c in range(k + 1, 8):
                    c_g[c] = c_g[c] - m * heads[k, c]
                lg = lg - m * pivots[k]
                rg = rg - m * marks[k]
            left[g], right[g] = lg, rg

def refresh_kernel(parts_ref, image_ref, panel_ref, values_ref, work, inverse, strip):
    num = sq = None
    for r in range(8):
        n_r = parts_ref[r * 640 + 576:r * 640 + 584, :]
        s_r = parts_ref[r * 640 + 584:r * 640 + 592, :]
        num = n_r if num is None else num + n_r
        sq = s_r if sq is None else sq + s_r
    values_ref[...] = num / (sq + 1e-06)
    for j in range(8):
        for i in range(j, 8):
            d = i - j
            if d == 4:
                block = jnp.concatenate([parts_ref[j * 640 + 512:j * 640 + 576, :], parts_ref[i * 640 + 512:i * 640 + 576, :]], axis=0).T
            elif d < 4:
                block = parts_ref[j * 640 + d * 128:j * 640 + d * 128 + 128, :]
                block = block.T if d else block
            else:
                block = parts_ref[i * 640 + (8 - d) * 128:i * 640 + (8 - d) * 128 + 128, :]
            work[j, i * 128:(i + 1) * 128, :] = block
        work[j, 1024:, :] = image_ref[j * 288:(j + 1) * 288, :]

    def step(j, carry):
        invert_block(work[j, pl.ds(pl.multiple_of(j * 128, 128), 128), :], inverse)
        for jj in range(8):
            @pl.when(j == jj)
            def _(jj=jj):
                top = (jj + 1) * 128
                strip[top:, :] = nt(work[jj, top:, :], inverse[...])
                panel_ref[:, jj * 128:(jj + 1) * 128] = strip[1024:, :]
                for k in range(jj + 1, 8):
                    work[k, k * 128:, :] -= nt(strip[k * 128:, :], strip[k * 128:(k + 1) * 128, :])
        return carry
    lax.fori_loop(0, 8, step, 0)

def refresh(parts, image):
    return pl.pallas_call(
        refresh_kernel,
        out_shape=(jax.ShapeDtypeStruct((288, 1024), jnp.float32), jax.ShapeDtypeStruct((8, 128), jnp.float32)),
        in_specs=[pl.BlockSpec(memory_space=pltpu.VMEM)] * 2,
        out_specs=(pl.BlockSpec(memory_space=pltpu.VMEM),) * 2,
        scratch_shapes=[pltpu.VMEM((8, 1312, 128), jnp.float32), pltpu.VMEM((128, 128), jnp.float32), pltpu.VMEM((1312, 128), jnp.float32)],
        compiler_params=pltpu.CompilerParams(vmem_limit_bytes=40 << 20),
        cost_estimate=pl.CostEstimate(flops=3 * 10**9, bytes_accessed=5 << 20, transcendentals=1024),
        name="refresh",
    )(parts, image)


def body(factor, panel):
    image, parts = combine(factor.reshape(BLOCK, 8 * BLOCK), panel.reshape(SHARD, 128))
    new_panel, values = refresh(
        parts.reshape(8 * SLICE, 128), image.reshape(8 * BLOCK, 128)
    )
    return (new_panel, values.reshape(1024))


def solution(mesh):
    placed = (P("blk", "rd", None), P(("blk", "rd"), None))
    return jax.shard_map(
        body, mesh=mesh, in_specs=placed, out_specs=(P("blk", None), P()), check_vma=False
    )
```

time: 1090 us -> 213 us (0.20)
  waiting for transfers between devices: 589 us -> 0 us
  other arithmetic: 269 us -> 0 us
  Pallas kernels: 0 us -> 208 us
  blocking collectives: 97.7 us -> 0 us
  matrix products: 55.5 us -> 0 us
  local copies, waits for them, and re-layouts: 54.3 us -> 4.38 us
  between operations: 19.9 us -> 0.64 us
    psum x1 -> x0, waiting for transfers between devices: 283 us -> none  [body(): lax.psum((inner_cols(left_cols, left_cols), inner_cols(left_cols, right_c...]
    another operation x33 -> x0, other arithmetic: 257 us -> none  [the longest x30 172 us: body(): lower = jnp.linalg.cholesky(gram)]
    all_gather x2 -> x0, waiting for transfers between devices: 234 us -> none  [the longest x1 234 us: body(): lax.all_gather(panel, 'blk', axis=0, tiled=True)]
    pallas_call x0 -> x2, Pallas kernels: none -> 208 us  [the longest x1 159 us: combine(): pl.pallas_call(combine_kernel, out_shape=(jax.ShapeDtypeStruct((Z, 2, BLO...]
    psum x1 -> x0, blocking collectives: 97.7 us -> none  [body(): lax.psum((jnp.sum(panel * image, axis=0), jnp.sum(panel * panel, axis=0))...]
    unnamed x5 -> x0, waiting for transfers between devices: 72.6 us -> none
    another operation x29 -> x0, matrix products: 34.1 us -> none  [the longest x14 23.1 us: body(): lower = jnp.linalg.cholesky(gram)]
    another operation x33 -> x0, local copies, waits for them, and re-layouts: 30.3 us -> none
  transfers between devices with their start and end apart: 4 -> 0, of which waited for: 3 -> 0; matrix products, arithmetic and copies ran while one was open for 0% -> 0% of each run, Pallas kernels for 0% -> 0%
where the time goes in v1:
time: 213 us
  Pallas kernels  208 us (98%)
  local copies, waits for them, and re-layouts  4.38 us (2%)
    pallas_call x1, Pallas kernels, combine(): pl.pallas_call(combine_kernel, out_shape=(jax.ShapeDtypeStruct((Z, 2, BLO...  159 us
    pallas_call x1, Pallas kernels, refresh(): pl.pallas_call(refresh_kernel, out_shape=(jax.ShapeDtypeStruct((288, 1024...  48.3 us

profile of v1, /device:TPU:1, one launch (start us, length us, event | category | flops | bytes accessed | tf_op | source)
XLA Modules:
  0.0 212.5 jit_solution(7963382376329714971)
XLA Ops:
  0.6 0.9 reshape.20.panel_ref
  1.6 3.4 %copy.6 = f32[288,1,2304]{2,0,1:T(8,128)} copy(f32[288,1,2304]{2,1,0:T(1,128)} %param.2) | data formatting | bytes 5308416
  5.0 159.2 %combine.1 = (f32[4,2,288,128]{3,2,1,0:T(8,128)S(1)}, f32[4,2,640,128]{3,2,1,0:T(8,128)S(1)}) custom-call(f32[288,2304]{1,0:T(8,128)} %bitcast.8, f32[288,128]{1,0:T(8,128)S(1)} %reshape.20.panel_ref), custom_call_target="tpu_custom_call" | custom-call | flops 5000000000 | bytes 8388608 | tf_op jit(solution)/shard_map/combine/pallas_call | solution.py:425
  164.3 48.3 %refresh.1 = (f32[288,1024]{1,0:T(8,128)}, f32[8,128]{1,0:T(8,128)}) custom-call(f32[5120,128]{1,0:T(8,128)S(1)} %bitcast.6, f32[2304,128]{1,0:T(8,128)S(1)} %bitcast.7), custom_call_target="tpu_custom_call" | custom-call | flops 3000000000 | bytes 5242880 | tf_op jit(solution)/shard_map/refresh/pallas_call | solution.py:536

commit v2 on v1

--- a/solution.py
+++ b/solution.py
@@ -16,16 +16,6 @@
 SLICE = 8 * CHUNK
 MESH = pl.DeviceIdType.MESH
 HIGHEST = lax.Precision.HIGHEST
-
-
-def nt(a, b):
-    return lax.dot_general(
-        a,
-        b,
-        (((1,), (1,)), ((), ())),
-        precision=HIGHEST,
-        preferred_element_type=jnp.float32,
-    )
 
 
 def ring(n):
@@ -148,8 +138,7 @@
     from_y,
     total_y,
     from_x,
-    total_x,
-    from_hi,
+    from_line,
     p_send,
     p_recv,
     r_send,
@@ -162,8 +151,6 @@
     x_recv,
     h_send,
     h_recv,
-    c_send,
-    c_recv,
     g_send,
     g_recv,
 ):
@@ -187,7 +174,10 @@
     def z_peer(d):
         return (blk, wrap(z + d, Z) * 2 + core)
 
-    hi_peer = (at_blk(1 - hi, x, y), rd)
+    def line_peer(d, e):
+        return (at_blk(1 - hi if e else hi, x, y), wrap(z + d, Z) * 2 + core)
+
+    hi_peer = line_peer(0, 1)
     core_peer = (blk, z * 2 + 1 - core)
 
     def remote(src, dst, send, recv, peer):
@@ -202,7 +192,7 @@
 
     barrier = pltpu.get_barrier_semaphore()
     peers = [x_peer(d) for d in range(1, X)] + [y_peer(d) for d in range(1, Y)]
-    peers += [z_peer(d) for d in range(1, Z)] + [hi_peer, core_peer]
+    peers += [line_peer(d, e) for e in range(2) for d in range(1 - e, Z)] + [core_peer]
     for peer in peers:
         pl.semaphore_signal(barrier, inc=1, device_id=peer, device_id_type=MESH)
 
@@ -240,7 +230,7 @@
 
                 def split(i, carry):
                     rows = pl.ds(pl.multiple_of(i * 16, 16), 16)
-                    value = factor_ref[rows, :]
+                    value = factor_ref[rows, 0, :]
                     top = value.astype(jnp.bfloat16)
                     high[rows, :] = top
                     low[rows, :] = (value - top.astype(jnp.float32)).astype(jnp.bfloat16)
@@ -331,18 +321,11 @@
     def _():
         local[512:576, :] = local[576:640, :]
 
-    def sums(i, carry):
-        numer, squares = carry
-        old = panel_ref[pl.ds(pl.multiple_of(i * 8, 8), 8), :]
-        new = jnp.concatenate(
-            [image_ref[g // 2, g % 2, pl.ds(rd * ROWS + i, 1), :] for g in range(8)], axis=0
-        )
-        return numer + old * new, squares + old * old
-
-    zero = jnp.zeros((8, 128), jnp.float32)
-    numer, squares = lax.fori_loop(0, ROWS, sums, (zero, zero))
-    local[576:584, :] = numer
-    local[584:592, :] = squares
+    for g in range(8):
+        old = panel_ref[pl.ds(g, ROWS, stride=8), :]
+        new = image_ref[g // 2, g % 2, pl.ds(rd * ROWS, ROWS), :]
+        local[576 + g : 577 + g, :] = jnp.sum(old * new, axis=0, keepdims=True)
+        local[584 + g : 585 + g, :] = jnp.sum(old * old, axis=0, keepdims=True)
     local[592:640, :] = jnp.zeros((48, 128), jnp.float32)
 
     def to_y(d):
@@ -373,24 +356,24 @@
         to_x(d, True).wait_recv()
     for d in range(1, X):
         to_x(d, False).wait_send()
-    total_x[...] = (from_x[0] + from_x[1]) + (from_x[2] + from_x[3])
-    to_hi = remote(total_x, from_hi, h_send.at[0], h_recv.at[0], hi_peer)
-    to_hi.start()
-    to_hi.wait()
+    from_line[z, hi] = (from_x[0] + from_x[1]) + (from_x[2] + from_x[3])
+
+    def to_line(d, e, arrived):
+        from_hi = 1 - hi if e and arrived else hi
+        where = from_line.at[wrap(z - d, Z) if arrived else z, from_hi]
+        slot = 2 * d + e
+        return remote(where, where, h_send.at[slot], h_recv.at[slot], line_peer(d, e))
+
+    line = [(d, e) for d in (2, 1, 3, 0) for e in (1, 0) if d or e]
+    for d, e in line:
+        to_line(d, e, False).start()
     here = pl.ds(pl.multiple_of(y * CHUNK, 8), CHUNK)
-    parts_ref[z, core, here, :] = (total_x[...] + from_hi[...]) * (1.0 / N)
-
-    def chunk_z(d, arrived):
-        who = wrap(z - d, Z) if arrived else z
-        where = parts_ref.at[who, core, here]
-        return remote(where, where, c_send.at[d - 1], c_recv.at[d - 1], z_peer(d))
-
-    for d in range(1, Z):
-        chunk_z(d, False).start()
-    for d in range(1, Z):
-        chunk_z(d, True).wait_recv()
-    for d in range(1, Z):
-        chunk_z(d, False).wait_send()
+    for d, e in line:
+        to_line(d, e, True).wait_recv()
+    for d, e in line:
+        to_line(d, e, False).wait_send()
+    for k in range(Z):
+        parts_ref[k, core, here, :] = (from_line[k, 0] + from_line[k, 1]) * (1.0 / N)
 
     def gram_copy(key, arrived):
         kind, sign, at, first, count = GRAM_META[key]
@@ -441,15 +424,13 @@
             pltpu.VMEM((Y - 1, CHUNK, 128), f32),
             pltpu.VMEM((CHUNK, 128), f32),
             pltpu.VMEM((X, CHUNK, 128), f32),
-            pltpu.VMEM((CHUNK, 128), f32),
-            pltpu.VMEM((CHUNK, 128), f32),
+            pltpu.VMEM((Z, 2, CHUNK, 128), f32),
             *pair(len(PANEL_MESSAGES)),
             *pair(Z),
             *pair(2 * Z),
             *pair(Y - 1),
             *pair(X - 1),
-            *pair(1),
-            *pair(Z - 1),
+            *pair(2 * Z),
             *pair(len(GRAM_MESSAGES)),
         ],
         compiler_params=pltpu.CompilerParams(
@@ -462,91 +443,148 @@
     )(factor, panel)
 
 
+def halves(value):
+    top = value.astype(jnp.bfloat16)
+    return top, (value - top.astype(jnp.float32)).astype(jnp.bfloat16)
+
+
+def nt(a, b):
+    def one(p, q):
+        return lax.dot_general(
+            p, q, (((1,), (1,)), ((), ())), preferred_element_type=jnp.float32
+        )
+
+    return one(a[1], b[0]) + one(a[0], b[1]) + one(a[0], b[0])
+
+
 def invert_block(a, out_ref):
     sub = lax.broadcasted_iota(jnp.int32, (8, 128), 0)
     lane = lax.broadcasted_iota(jnp.int32, (8, 128), 1)
-    left = [a[8 * g:8 * g + 8, :] for g in range(16)]
+    left = [a[8 * g : 8 * g + 8, :] for g in range(16)]
     right = [jnp.where(lane == sub + 8 * g, 1.0, 0.0) for g in range(16)]
+
     def column(tile, at):
-        return jnp.broadcast_to(tile[:, at:at + 1], (8, 128))
+        return jnp.broadcast_to(tile[:, at : at + 1], (8, 128))
+
     def row(tile, at):
-        return jnp.broadcast_to(tile[at:at + 1, :], (8, 128))
+        return jnp.broadcast_to(tile[at : at + 1, :], (8, 128))
+
     for p in range(16):
-        at, eye = left[p], right[p]
-        cols = [column(at, 8 * p + k) for k in range(8)]
+        here, eye = left[p], right[p]
+        cols = [column(here, 8 * p + k) for k in range(8)]
         heads, recips, pivots, marks = {}, [], [], []
         for k in range(8):
             d = row(cols[k], k)
             r = 1.0 / d
             m = jnp.where(sub > k, cols[k] * r, 0.0)
-            u, w = row(at, k), row(eye, k)
-            out_ref[8 * p + k:8 * p + k + 1, :] = (w * lax.rsqrt(d))[0:1, :]
+            u, w = row(here, k), row(eye, k)
+            out_ref[8 * p + k : 8 * p + k + 1, :] = (w * lax.rsqrt(d))[0:1, :]
             for c in range(k + 1, 8):
                 heads[k, c] = row(cols[c], k)
                 cols[c] = cols[c] - m * heads[k, c]
-            at = at - m * u
+            here = here - m * u
             eye = eye - m * w
-            recips.append(r); pivots.append(u); marks.append(w)
+            recips.append(r)
+            pivots.append(u)
+            marks.append(w)
         for g in range(p + 1, 16):
-            c_g = [column(left[g], 8 * p + k) for k in range(8)]
+            tall = [column(left[g], 8 * p + k) for k in range(8)]
             lg, rg = left[g], right[g]
             for k in range(8):
-                m = c_g[k] * recips[k]
+                m = tall[k] * recips[k]
                 for c in range(k + 1, 8):
-                    c_g[c] = c_g[c] - m * heads[k, c]
+                    tall[c] = tall[c] - m * heads[k, c]
                 lg = lg - m * pivots[k]
                 rg = rg - m * marks[k]
             left[g], right[g] = lg, rg
 
-def refresh_kernel(parts_ref, image_ref, panel_ref, values_ref, work, inverse, strip):
+
+TALL = 1024 + BLOCK
+PIECE = TALL // 4
+
+
+def refresh_kernel(
+    parts_ref, image_ref, panel_ref, values_ref, work, rest, high, low, inverse, w_high, w_low
+):
     num = sq = None
     for r in range(8):
-        n_r = parts_ref[r * 640 + 576:r * 640 + 584, :]
-        s_r = parts_ref[r * 640 + 584:r * 640 + 592, :]
+        at = r * SLICE + 576
+        n_r, s_r = parts_ref[at : at + 8, :], parts_ref[at + 8 : at + 16, :]
         num = n_r if num is None else num + n_r
         sq = s_r if sq is None else sq + s_r
     values_ref[...] = num / (sq + 1e-06)
     for j in range(8):
         for i in range(j, 8):
-            d = i - j
+            d, at, far = i - j, j * SLICE, i * SLICE
             if d == 4:
-                block = jnp.concatenate([parts_ref[j * 640 + 512:j * 640 + 576, :], parts_ref[i * 640 + 512:i * 640 + 576, :]], axis=0).T
+                block = jnp.concatenate(
+                    [parts_ref[at + 512 : at + 576, :], parts_ref[far + 512 : far + 576, :]],
+                    axis=0,
+                ).T
             elif d < 4:
-                block = parts_ref[j * 640 + d * 128:j * 640 + d * 128 + 128, :]
+                block = parts_ref[at + d * 128 : at + d * 128 + 128, :]
                 block = block.T if d else block
             else:
-                block = parts_ref[i * 640 + (8 - d) * 128:i * 640 + (8 - d) * 128 + 128, :]
-            work[j, i * 128:(i + 1) * 128, :] = block
-        work[j, 1024:, :] = image_ref[j * 288:(j + 1) * 288, :]
+                block = parts_ref[far + (8 - d) * 128 : far + (8 - d) * 128 + 128, :]
+            work[j, i * 128 : (i + 1) * 128, :] = block
+        work[j, 1024:, :] = image_ref[j * BLOCK : (j + 1) * BLOCK, :]
+    high[...] = jnp.zeros_like(high)
+    low[...] = jnp.zeros_like(low)
+    rest[...] = jnp.zeros_like(rest)
+    inverse[...] = jnp.zeros_like(inverse)
 
     def step(j, carry):
-        invert_block(work[j, pl.ds(pl.multiple_of(j * 128, 128), 128), :], inverse)
-        for jj in range(8):
-            @pl.when(j == jj)
-            def _(jj=jj):
-                top = (jj + 1) * 128
-                strip[top:, :] = nt(work[jj, top:, :], inverse[...])
-                panel_ref[:, jj * 128:(jj + 1) * 128] = strip[1024:, :]
-                for k in range(jj + 1, 8):
-                    work[k, k * 128:, :] -= nt(strip[k * 128:, :], strip[k * 128:(k + 1) * 128, :])
+        done = pl.ds(pl.multiple_of(jnp.maximum(j - 1, 0) * 128, 128), 128)
+        rows = pl.ds(pl.multiple_of(j * 128, 128), 128)
+        before = halves(inverse[...])
+        w_high[...], w_low[...] = before
+        strip = halves(nt(halves(rest[rows, :]), before))
+        high[rows, done], low[rows, done] = strip
+        side = (high[rows, :], low[rows, :])
+        invert_block(work[j, rows, :] - nt(side, side), inverse)
+        for n in range(4):
+            span = slice(n * PIECE, (n + 1) * PIECE)
+            solved = nt(halves(rest[span, :]), (w_high[...], w_low[...]))
+            if n == 3:
+                panel_ref[:, done] = solved[PIECE - BLOCK :, :]
+            high[span, done], low[span, done] = halves(solved)
+            rest[span, :] = work[j, span, :] - nt((high[span, :], low[span, :]), side)
         return carry
+
     lax.fori_loop(0, 8, step, 0)
+    panel_ref[:, 896:] = nt(halves(rest[1024:, :]), halves(inverse[...]))
+
 
 def refresh(parts, image):
+    f32, bf16 = jnp.float32, jnp.bfloat16
+    vmem = pl.BlockSpec(memory_space=pltpu.VMEM)
     return pl.pallas_call(
         refresh_kernel,
-        out_shape=(jax.ShapeDtypeStruct((288, 1024), jnp.float32), jax.ShapeDtypeStruct((8, 128), jnp.float32)),
-        in_specs=[pl.BlockSpec(memory_space=pltpu.VMEM)] * 2,
-        out_specs=(pl.BlockSpec(memory_space=pltpu.VMEM),) * 2,
-        scratch_shapes=[pltpu.VMEM((8, 1312, 128), jnp.float32), pltpu.VMEM((128, 128), jnp.float32), pltpu.VMEM((1312, 128), jnp.float32)],
-        compiler_params=pltpu.CompilerParams(vmem_limit_bytes=40 << 20),
-        cost_estimate=pl.CostEstimate(flops=3 * 10**9, bytes_accessed=5 << 20, transcendentals=1024),
+        out_shape=(
+            jax.ShapeDtypeStruct((BLOCK, 1024), f32),
+            jax.ShapeDtypeStruct((8, 128), f32),
+        ),
+        in_specs=[vmem, vmem],
+        out_specs=(vmem, vmem),
+        scratch_shapes=[
+            pltpu.VMEM((8, TALL, 128), f32),
+            pltpu.VMEM((TALL, 128), f32),
+            pltpu.VMEM((TALL, 1024), bf16),
+            pltpu.VMEM((TALL, 1024), bf16),
+            pltpu.VMEM((128, 128), f32),
+            pltpu.VMEM((128, 128), bf16),
+            pltpu.VMEM((128, 128), bf16),
+        ],
+        compiler_params=pltpu.CompilerParams(vmem_limit_bytes=48 << 20),
+        cost_estimate=pl.CostEstimate(
+            flops=3 * 10**9, bytes_accessed=5 << 20, transcendentals=1024
+        ),
         name="refresh",
     )(parts, image)
 
 
 def body(factor, panel):
-    image, parts = combine(factor.reshape(BLOCK, 8 * BLOCK), panel.reshape(SHARD, 128))
+    image, parts = combine(factor, panel.reshape(SHARD, 128))
     new_panel, values = refresh(
         parts.reshape(8 * SLICE, 128), image.reshape(8 * BLOCK, 128)
     )

time: 213 us -> 205 us (0.962)
  Pallas kernels: 208 us -> 203 us
  local copies, waits for them, and re-layouts: 4.38 us -> 0.94 us
    pallas_call x1, Pallas kernels: 48.3 us -> 42.1 us  [refresh(): pl.pallas_call(refresh_kernel, out_shape=(jax.ShapeDtypeStruct((BLOCK, 10...]
    unnamed x1 -> x0, local copies, waits for them, and re-layouts: 3.43 us -> none
where the time goes in v2:
time: 205 us
  Pallas kernels  203 us (99%)
    pallas_call x1, Pallas kernels, combine(): pl.pallas_call(combine_kernel, out_shape=(jax.ShapeDtypeStruct((Z, 2, BLO...  161 us
    pallas_call x1, Pallas kernels, refresh(): pl.pallas_call(refresh_kernel, out_shape=(jax.ShapeDtypeStruct((BLOCK, 10...  42.1 us

profile of v2, /device:TPU:1, one launch (start us, length us, event | category | flops | bytes accessed | tf_op | source)
XLA Modules:
  0.0 204.6 jit_solution(9992634516135906637)
XLA Ops:
  0.6 0.9 reshape.16.panel_ref
  1.6 160.8 %combine.1 = (f32[4,2,288,128]{3,2,1,0:T(8,128)S(1)}, f32[4,2,640,128]{3,2,1,0:T(8,128)S(1)}) custom-call(f32[288,1,2304]{2,1,0:T(1,128)} %factor_ref.1, f32[288,128]{1,0:T(8,128)S(1)} %reshape.16.panel_ref), custom_call_target="tpu_custom_call" | custom-call | flops 5000000000 | bytes 8388608 | tf_op jit(solution)/shard_map/combine/pallas_call | solution.py:408
  162.4 42.1 %refresh.1 = (f32[288,1024]{1,0:T(8,128)}, f32[8,128]{1,0:T(8,128)}) custom-call(f32[5120,128]{1,0:T(8,128)S(1)} %bitcast.3, f32[2304,128]{1,0:T(8,128)S(1)} %bitcast.4), custom_call_target="tpu_custom_call" | custom-call | flops 3000000000 | bytes 5242880 | tf_op jit(solution)/shard_map/refresh/pallas_call | solution.py:561

commit v3 on v2

--- a/solution.py
+++ b/solution.py
@@ -10,7 +10,8 @@
 N = 18432
 X, Y, Z = 4, 8, 4
 ROWS = 36
-SHARD = ROWS * 8
+HALF = ROWS * 4
+SIDE = X * Y * HALF
 BLOCK = 288
 CHUNK = 80
 SLICE = 8 * CHUNK
@@ -18,81 +19,138 @@
 HIGHEST = lax.Precision.HIGHEST
 
 
-def ring(n):
+def ring(n, whole=0):
     h = n // 2
     for sign in (1, -1):
         for t in range(h - 1):
             yield sign, sign * t, None
-        yield sign, sign * (h - 1), 0 if sign > 0 else 1
-
-
-def order(messages, preset=()):
-    waiting = {k: set(m[3]) - set(preset) for k, m in messages.items()}
+        if whole == 0:
+            yield sign, sign * (h - 1), 0 if sign > 0 else 1
+        elif whole == sign:
+            yield sign, sign * (h - 1), None
+
+
+def order(nodes, ahead=2.0):
+    waiting = {k: set(v[3]) for k, v in nodes.items()}
     followers = {}
-    for k, m in messages.items():
-        for d in m[3]:
+    for k, v in nodes.items():
+        for d in set(v[3]):
             followers.setdefault(d, []).append(k)
-    free, heap, events = {}, [], []
-
-    def start(k, now):
-        link, size, latency, _ = messages[k]
-        begin = max(now, free.get(link, 0.0))
-        free[link] = begin + size
-        events.append(("start", k))
-        heapq.heappush(heap, (begin + size + latency, len(events), k))
-
-    for k in messages:
+    free, queues, heap, events = {}, {}, [], []
+    place = {k: i for i, k in enumerate(nodes)}
+
+    def push(when, kind, what):
+        push.count += 1
+        heapq.heappush(heap, (when, push.count, kind, what))
+
+    push.count = 0
+
+    def pump(resource, now):
+        queue = queues.setdefault(resource, [])
+        reach = 0.0 if resource == "tc" else ahead
+        while queue and free.get(resource, 0.0) - now <= reach:
+            key = heapq.heappop(queue)[2]
+            begin = max(now, free.get(resource, 0.0))
+            free[resource] = begin + nodes[key][1]
+            events.append(("task" if resource == "tc" else "start", key))
+            push(free[resource] + nodes[key][2], "done", key)
+        if queue:
+            push(free[resource] - reach, "pump", resource)
+
+    def ready(key, now):
+        heapq.heappush(queues.setdefault(nodes[key][0], []), (nodes[key][4], place[key], key))
+        pump(nodes[key][0], now)
+
+    for k in nodes:
         if not waiting[k]:
-            start(k, 0.0)
+            ready(k, 0.0)
     while heap:
-        now, _, k = heapq.heappop(heap)
-        events.append(("wait", k))
-        for f in followers.get(k, ()):
-            waiting[f].discard(k)
+        now, _, kind, what = heapq.heappop(heap)
+        if kind == "pump":
+            pump(what, now)
+            continue
+        if nodes[what][0] != "tc":
+            events.append(("wait", what))
+        for f in followers.get(what, ()):
+            waiting[f].discard(what)
             if not waiting[f]:
-                start(f, now)
-    assert sum(e == "start" for e, _ in events) == len(messages)
+                ready(f, now)
+    assert not any(waiting.values())
     return events
 
 
-def panel_messages():
+SPLITS = 6
+
+
+def image_nodes():
     rate = 50e3
-    out = {}
-    meta = {}
-    z_key = ("z",)
-    out[z_key] = ("z", SHARD * 512 / 25e3, 3.0, ())
-    meta[z_key] = ("z", 0, 0, 0, 0, SHARD)
-    for z in range(2):
-        base = (z_key,) if z else ()
+    out, meta = {}, {}
+    splits = tuple(("split", i) for i in range(SPLITS))
+    products = {0: [], 1: []}
+    early = []
+    for unit, (h, far) in enumerate(((0, 0), (0, 1), (1, 2))):
+        needs = ()
+        if far:
+            z_key = ("hi", h)
+            out[z_key] = ("z", HALF * 1024 / 50e3, 3.0, (), h)
+            meta[z_key] = ("hi", h, 0, 0, 0, 0, 0, HALF)
+            needs = (z_key,)
+        wide = 2 if far == 2 else 1
+        arrivals = []
         for part, (first, rows) in enumerate(((0, 22), (22, 14))):
             axes = (("y", Y), ("x", X)) if part == 0 else (("x", X), ("y", Y))
             (f_name, f_n), (s_name, s_n) = axes
-            half = rows // 2
+            big = (rows // 2 + 1) // 2 * 2
 
             def cut(piece):
-                return (first, rows) if piece is None else (first + piece * half, half)
-
-            def offset(f, s):
-                return (f, s) if f_name == "x" else (s, f)
-
-            delivered = {0: base}
+                if piece is None:
+                    return first, rows
+                return (first, big) if piece == 0 else (first + big, rows - big)
+
+            def send(key, name, sign, f, s, piece, dep):
+                start, count = cut(piece)
+                ox, oy = (f, s) if f_name == "x" else (s, f)
+                took = count * 4 * 512 * wide / rate
+                out[key] = (name + str(sign), took, 1.0, dep, 2 * unit + (key[3] != "f"))
+                meta[key] = (name, h, far, sign, ox, oy, start * 4, count * 4)
+                arrivals.append(key)
+
+            delivered = {0: needs}
             for sign, at, piece in ring(f_n):
-                key = (z, part, "f", 0, sign, at)
-                dep = base if at == 0 else ((z, part, "f", 0, sign, at - sign),)
-                start, count = cut(piece)
-                ox, oy = offset(at, 0)
-                out[key] = (f_name + str(sign), count * 4096 / rate, 1.0, dep)
-                meta[key] = (f_name, sign, z, ox, oy, start * 8, count * 8)
+                key = (unit, part, sign, "f", 0, at)
+                dep = needs if at == 0 else ((unit, part, sign, "f", 0, at - sign),)
+                send(key, f_name, sign, at, 0, piece, dep)
                 to = (at + sign) % f_n
                 delivered[to] = delivered.get(to, ()) + (key,)
             for f in sorted(delivered, key=lambda v: min(v, f_n - v)):
-                for sign, at, piece in ring(s_n):
-                    key = (z, part, "s", f, sign, at)
-                    dep = delivered[f] if at == 0 else ((z, part, "s", f, sign, at - sign),)
-                    start, count = cut(piece)
-                    ox, oy = offset(f, at)
-                    out[key] = (s_name + str(sign), count * 4096 / rate, 1.0, dep)
-                    meta[key] = (s_name, sign, z, ox, oy, start * 8, count * 8)
+                for sign, at, piece in ring(s_n, 1 if f % 2 == 0 else -1):
+                    key = (unit, part, sign, "s", f, at)
+                    dep = (
+                        delivered[f] if at == 0 else ((unit, part, sign, "s", f, at - sign),)
+                    )
+                    send(key, s_name, sign, f, at, piece, dep)
+        if unit == 0:
+            early = arrivals
+        for side in (far,) if far < 2 else (0, 1):
+            for q in range(2):
+                key = ("product", h, side, q)
+                out[key] = ("tc", 0.8, 0.0, needs + tuple(arrivals) + splits, 0)
+                products[h].append(key)
+    for i, key in enumerate(splits):
+        out[key] = ("tc", 0.5, 0.0, (early[4 + 6 * i],), 1)
+    for h in range(2):
+        out["core", h] = ("c", 0.7, 1.0, tuple(products[h]), 0)
+        out["add", h] = ("tc", 0.3, 0.0, (("core", h),), 0)
+        out["own", h] = ("tc", 0.2, 0.0, tuple(("sum", h, d) for d in range(1, Z)), 0)
+        for d in (2, 1, 3):
+            out["sum", h, d] = ("zz", 2.0, 1.5, (("add", h),), 0)
+            out["spread", h, d] = ("zz", 2.0, 1.5, (("own", h),), 0)
+        for d in range(Z):
+            dep = ("spread", h, d) if d else ("own", h)
+            out["share", h, d] = ("c", 0.2, 0.7, (dep,), 0)
+    for key in out:
+        if key not in meta and out[key][0] != "tc":
+            meta[key] = key
     return out, meta
 
 
@@ -104,20 +162,20 @@
         key = ("y", sign, at)
         dep = () if at == 0 else (("y", sign, at - sign),)
         first, count = (0, Z) if piece is None else (piece * Z // 2, Z // 2)
-        out[key] = ("y" + str(sign), count * CHUNK * 512 / 50e3, 1.0, dep)
+        out[key] = ("y" + str(sign), count * CHUNK * 512 / 50e3, 1.0, dep, 0)
         meta[key] = ("y", sign, at, first, count)
         to = (at + sign) % Y
         delivered[to] = delivered.get(to, ()) + (key,)
     for f, dep in delivered.items():
         key = ("core", f)
-        out[key] = ("core", Z * CHUNK * 512 / 400e3, 0.5, dep)
+        out[key] = ("core", Z * CHUNK * 512 / 400e3, 0.5, dep, 0)
         meta[key] = ("core", 0, f, 0, Z)
     return out, meta
 
 
-PANEL_MESSAGES, PANEL_META = panel_messages()
-PANEL_EVENTS = order(PANEL_MESSAGES)
-PANEL_SLOT = {k: i for i, k in enumerate(PANEL_MESSAGES)}
+IMAGE_NODES, IMAGE_META = image_nodes()
+IMAGE_EVENTS = order(IMAGE_NODES)
+IMAGE_SLOT = {k: i for i, k in enumerate(IMAGE_META)}
 GRAM_MESSAGES, GRAM_META = gram_messages()
 GRAM_EVENTS = order(GRAM_MESSAGES)
 GRAM_SLOT = {k: i for i, k in enumerate(GRAM_MESSAGES)}
@@ -141,10 +199,6 @@
     from_line,
     p_send,
     p_recv,
-    r_send,
-    r_recv,
-    a_send,
-    a_recv,
     y_send,
     y_recv,
     x_send,
@@ -196,113 +250,94 @@
     for peer in peers:
         pl.semaphore_signal(barrier, inc=1, device_id=peer, device_id_type=MESH)
 
-    own = pl.multiple_of(blk * SHARD, 8)
-    gathered[pl.ds(own, SHARD), :] = panel_ref[...]
+    own = pl.ds(pl.multiple_of((x * Y + y) * HALF, 8), HALF)
+    for h in range(2):
+        gathered[h, hi, own, :] = panel_ref[h]
     pl.semaphore_wait(barrier, len(peers))
 
-    def panel_copy(key, arrived):
-        axis, sign, far, ox, oy, *span = PANEL_META[key]
-        slot = PANEL_SLOT[key]
-        if axis == "z":
-            peer = hi_peer
-            source = 1 - hi if arrived else hi
-            start, count = 0, SHARD
-            origin = at_blk(source, x, y)
+    my_rows = pl.ds(pl.multiple_of(core * (BLOCK // 2), 8), BLOCK // 2)
+    other_rows = pl.ds(pl.multiple_of((1 - core) * (BLOCK // 2), 8), BLOCK // 2)
+
+    def image_copy(key, arrived):
+        kind, h, *more = IMAGE_META[key]
+        if kind in ("x", "y", "hi"):
+            far, sign, ox, oy, start, count = more
+            if kind == "hi":
+                peer = hi_peer
+                side = 1 - hi if arrived else hi
+            else:
+                peer = x_peer(sign) if kind == "x" else y_peer(sign)
+                side = (hi, 1 - hi, slice(None))[far]
+                if arrived:
+                    ox, oy = (ox + sign, oy) if kind == "x" else (ox, oy + sign)
+            origin = wrap(x - ox % X, X) * Y + wrap(y - oy % Y, Y)
+            rows = pl.ds(pl.multiple_of(origin * HALF + start, 8), count)
+            src = dst = gathered.at[h, side, rows]
+        elif kind == "core":
+            peer = core_peer
+            src, dst = partial.at[h, :, other_rows], from_core.at[h]
+        elif kind == "sum":
+            d = more[0]
+            peer = z_peer(d)
+            src, dst = from_core.at[h, wrap(z + d, Z)], from_z.at[h, d - 1]
+        elif kind == "spread":
+            d = more[0]
+            peer = z_peer(d)
+            src = dst = image_ref.at[4 * h + (wrap(z - d, Z) if arrived else z), my_rows]
         else:
-            peer = x_peer(sign) if axis == "x" else y_peer(sign)
-            start, count = span
-            if arrived:
-                ox, oy = (ox + sign, oy) if axis == "x" else (ox, oy + sign)
-            source = 1 - hi if far else hi
-            origin = at_blk(source, wrap(x - ox % X, X), wrap(y - oy % Y, Y))
-        where = pl.ds(pl.multiple_of(origin * SHARD + start, 8), count)
-        return remote(
-            gathered.at[where], gathered.at[where], p_send.at[slot], p_recv.at[slot], peer
+            d = more[0]
+            peer = core_peer
+            rows = other_rows if arrived else my_rows
+            src = dst = image_ref.at[4 * h + wrap(z - d, Z), rows]
+        slot = IMAGE_SLOT[key]
+        return remote(src, dst, p_send.at[slot], p_recv.at[slot], peer)
+
+    def split(i):
+        count = BLOCK // SPLITS
+        rows = slice(i * count, (i + 1) * count)
+        value = factor_ref[rows, 0, :]
+        high[rows, :], low[rows, :] = halves(value)
+
+    def product(h, far, q):
+        side = 1 - hi if far else hi
+        right = jnp.concatenate(
+            [gathered[h, side, pl.ds(2 * q + s, SIDE // 4, stride=4), :] for s in range(2)],
+            axis=1,
         )
-
-    started = 0
-    for event, key in PANEL_EVENTS:
+        top, rest = halves(right)
+        span = pl.ds(pl.multiple_of(side * (SIDE // 4), 128), SIDE // 4)
+        value = (
+            jnp.dot(low[:, span], top, preferred_element_type=jnp.float32)
+            + jnp.dot(high[:, span], rest, preferred_element_type=jnp.float32)
+            + jnp.dot(high[:, span], top, preferred_element_type=jnp.float32)
+        )
+        for s in range(2):
+            piece = value[:, s * 128 : s * 128 + 128]
+            if far:
+                piece = partial[h, 2 * q + s] + piece
+            partial[h, 2 * q + s] = piece
+
+    def add(h):
+        for k in range(Z):
+            from_core[h, k] += partial[h, k, my_rows, :]
+
+    def own_sum(h):
+        value = from_core[h, z] + from_z[h, 0] + from_z[h, 1] + from_z[h, 2]
+        image_ref[4 * h + z, my_rows, :] = value
+
+    tasks = dict(split=split, product=product, add=add, own=own_sum)
+    for event, key in IMAGE_EVENTS:
         if event == "start":
-            panel_copy(key, False).start()
+            image_copy(key, False).start()
+        elif event == "wait":
+            image_copy(key, True).wait_recv()
         else:
-            if started == 0:
-                started = 1
-
-                def split(i, carry):
-                    rows = pl.ds(pl.multiple_of(i * 16, 16), 16)
-                    value = factor_ref[rows, 0, :]
-                    top = value.astype(jnp.bfloat16)
-                    high[rows, :] = top
-                    low[rows, :] = (value - top.astype(jnp.float32)).astype(jnp.bfloat16)
-                    return carry
-
-                lax.fori_loop(0, BLOCK // 16, split, 0)
-            panel_copy(key, True).wait_recv()
-    for key in PANEL_MESSAGES:
-        panel_copy(key, False).wait_send()
-
-    for q in range(4):
-        right = jnp.concatenate(
-            [gathered[pl.ds(2 * q + s, 8 * BLOCK, stride=8), :] for s in range(2)], axis=1
-        )
-        r_top = right.astype(jnp.bfloat16)
-        r_low = (right - r_top.astype(jnp.float32)).astype(jnp.bfloat16)
-        product = (
-            jnp.dot(low[...], r_top, preferred_element_type=jnp.float32)
-            + jnp.dot(high[...], r_low, preferred_element_type=jnp.float32)
-            + jnp.dot(high[...], r_top, preferred_element_type=jnp.float32)
-        )
-        partial[q, 0] = product[:, :128]
-        partial[q, 1] = product[:, 128:]
-
-    to_core = remote(
-        partial.at[:, 1 - core], from_core, r_send.at[0], r_recv.at[0], core_peer
-    )
-    to_core.start()
-    to_core.wait()
-    for k in range(Z):
-        from_core[k] += partial[k, core]
-    to_z = [
-        remote(
-            from_core.at[wrap(z + d, Z)],
-            from_z.at[d - 1],
-            r_send.at[d],
-            r_recv.at[d],
-            z_peer(d),
-        )
-        for d in range(1, Z)
-    ]
-    for copy in to_z:
-        copy.start()
-    for copy in to_z:
-        copy.wait()
-    image_ref[z, core] = from_core[z] + from_z[0] + from_z[1] + from_z[2]
-
-    def spread(d, arrived):
-        who = wrap(z - d, Z) if arrived else z
-        where = image_ref.at[who, core]
-        return remote(where, where, a_send.at[d], a_recv.at[d], z_peer(d))
-
-    def share(k, arrived):
-        who = wrap(z - k, Z)
-        where = image_ref.at[who, 1 - core if arrived else core]
-        return remote(where, where, a_send.at[Z + k], a_recv.at[Z + k], core_peer)
-
-    for d in range(1, Z):
-        spread(d, False).start()
-    share(0, False).start()
-    for d in range(1, Z):
-        spread(d, True).wait_recv()
-        share(d, False).start()
-    for d in range(Z):
-        share(d, True).wait_recv()
-    for d in range(1, Z):
-        spread(d, False).wait_send()
-    for d in range(Z):
-        share(d, False).wait_send()
+            tasks[key[0]](*key[1:])
+    for key in IMAGE_META:
+        image_copy(key, False).wait_send()
 
     def group(g):
-        return image_ref[g // 2, g % 2]
+        return image_ref[g]
 
     mine = group(rd).T
     for d in range(4):
@@ -322,8 +357,8 @@
         local[512:576, :] = local[576:640, :]
 
     for g in range(8):
-        old = panel_ref[pl.ds(g, ROWS, stride=8), :]
-        new = image_ref[g // 2, g % 2, pl.ds(rd * ROWS, ROWS), :]
+        old = panel_ref[g // 4, pl.ds(g % 4, ROWS, stride=4), :]
+        new = image_ref[g, pl.ds(rd * ROWS, ROWS), :]
         local[576 + g : 577 + g, :] = jnp.sum(old * new, axis=0, keepdims=True)
         local[584 + g : 585 + g, :] = jnp.sum(old * old, axis=0, keepdims=True)
     local[592:640, :] = jnp.zeros((48, 128), jnp.float32)
@@ -408,26 +443,24 @@
     return pl.pallas_call(
         combine_kernel,
         out_shape=(
-            jax.ShapeDtypeStruct((Z, 2, BLOCK, 128), f32),
+            jax.ShapeDtypeStruct((8, BLOCK, 128), f32),
             jax.ShapeDtypeStruct((Z, 2, SLICE, 128), f32),
         ),
         in_specs=[vmem, vmem],
         out_specs=(vmem, vmem),
         scratch_shapes=[
-            pltpu.VMEM((64 * SHARD, 128), f32),
+            pltpu.VMEM((2, 2, SIDE, 128), f32),
             pltpu.VMEM((BLOCK, 8 * BLOCK), bf16),
             pltpu.VMEM((BLOCK, 8 * BLOCK), bf16),
-            pltpu.VMEM((Z, 2, BLOCK, 128), f32),
-            pltpu.VMEM((Z, BLOCK, 128), f32),
-            pltpu.VMEM((Z - 1, BLOCK, 128), f32),
+            pltpu.VMEM((2, Z, BLOCK, 128), f32),
+            pltpu.VMEM((2, Z, BLOCK // 2, 128), f32),
+            pltpu.VMEM((2, Z - 1, BLOCK // 2, 128), f32),
             pltpu.VMEM((SLICE, 128), f32),
             pltpu.VMEM((Y - 1, CHUNK, 128), f32),
             pltpu.VMEM((CHUNK, 128), f32),
             pltpu.VMEM((X, CHUNK, 128), f32),
             pltpu.VMEM((Z, 2, CHUNK, 128), f32),
-            *pair(len(PANEL_MESSAGES)),
-            *pair(Z),
-            *pair(2 * Z),
+            *pair(len(IMAGE_META)),
             *pair(Y - 1),
             *pair(X - 1),
             *pair(2 * Z),
@@ -584,7 +617,9 @@
 
 
 def body(factor, panel):
-    image, parts = combine(factor, panel.reshape(SHARD, 128))
+    image, parts = combine(
+        factor, panel.reshape(ROWS, 2, 4, 128).transpose(1, 0, 2, 3).reshape(2, HALF, 128)
+    )
     new_panel, values = refresh(
         parts.reshape(8 * SLICE, 128), image.reshape(8 * BLOCK, 128)
     )

time: 205 us -> 199 us (0.971)
  Pallas kernels: 203 us -> 197 us
    pallas_call x1, Pallas kernels: 161 us -> 155 us  [combine(): pl.pallas_call(combine_kernel, out_shape=(jax.ShapeDtypeStruct((8, BLOCK,...]
where the time goes in v3:
time: 199 us; the launch traced here: 198 us
  Pallas kernels  197 us (99%)
    pallas_call x1, Pallas kernels, combine(): pl.pallas_call(combine_kernel, out_shape=(jax.ShapeDtypeStruct((8, BLOCK,...  155 us
    pallas_call x1, Pallas kernels, refresh(): pl.pallas_call(refresh_kernel, out_shape=(jax.ShapeDtypeStruct((BLOCK, 10...  42.1 us

profile of v3, /device:TPU:1, one launch (start us, length us, event | category | flops | bytes accessed | tf_op | source)
XLA Modules:
  0.0 198.3 jit_solution(6759528856335633724)
XLA Ops:
  0.6 1.0 reshape.19
  1.7 154.5 %combine.1 = (f32[8,288,128]{2,1,0:T(8,128)S(1)}, f32[4,2,640,128]{3,2,1,0:T(8,128)S(1)}) custom-call(f32[288,1,2304]{2,1,0:T(1,128)} %factor_ref.1, f32[2,144,128]{2,1,0:T(8,128)S(1)} %bitcast.6), custom_call_target="tpu_custom_call" | custom-call | flops 5000000000 | bytes 8388608 | tf_op jit(solution)/shard_map/combine/pallas_call | solution.py:443
  156.2 42.1 %refresh.1 = (f32[288,1024]{1,0:T(8,128)}, f32[8,128]{1,0:T(8,128)}) custom-call(f32[5120,128]{1,0:T(8,128)S(1)} %bitcast.7, f32[2304,128]{1,0:T(8,128)S(1)} %bitcast.8), custom_call_target="tpu_custom_call" | custom-call | flops 3000000000 | bytes 5242880 | tf_op jit(solution)/shard_map/refresh/pallas_call | solution.py:594
  (1 shorter events, 0.0 us)

commit v4 on v3

--- a/solution.py
+++ b/solution.py
@@ -13,8 +13,9 @@
 HALF = ROWS * 4
 SIDE = X * Y * HALF
 BLOCK = 288
-CHUNK = 80
-SLICE = 8 * CHUNK
+CHUNK = 24
+SLICE = X * Y * CHUNK
+X_ROWS = Y * CHUNK
 MESH = pl.DeviceIdType.MESH
 HIGHEST = lax.Precision.HIGHEST
 
@@ -154,31 +155,46 @@
     return out, meta
 
 
-def gram_messages():
-    out = {}
-    meta = {}
-    delivered = {0: ()}
-    for sign, at, piece in ring(Y):
-        key = ("y", sign, at)
-        dep = () if at == 0 else (("y", sign, at - sign),)
-        first, count = (0, Z) if piece is None else (piece * Z // 2, Z // 2)
-        out[key] = ("y" + str(sign), count * CHUNK * 512 / 50e3, 1.0, dep, 0)
-        meta[key] = ("y", sign, at, first, count)
-        to = (at + sign) % Y
-        delivered[to] = delivered.get(to, ()) + (key,)
-    for f, dep in delivered.items():
-        key = ("core", f)
-        out[key] = ("core", Z * CHUNK * 512 / 400e3, 0.5, dep, 0)
-        meta[key] = ("core", 0, f, 0, Z)
+def gram_nodes():
+    rate = 50e3
+    out, meta, blocks = {}, {}, {}
+    for part, (first, rows) in enumerate(((0, 16), (16, 8))):
+        axes = (("y", Y), ("x", X)) if part == 0 else (("x", X), ("y", Y))
+        (f_name, f_n), (s_name, s_n) = axes
+
+        def send(key, name, sign, f, s, piece, dep):
+            start, count = (first, rows) if piece is None else (first + 8 * piece, 8)
+            ox, oy = (f, s) if f_name == "x" else (s, f)
+            took = Z * count * 512 / rate
+            out[key] = (name + str(sign), took, 1.0, dep, int(key[2] != "f"))
+            meta[key] = (name, sign, ox, oy, start, count)
+            to = (ox + sign) % X if name == "x" else ox % X
+            blocks.setdefault(to, []).append(key)
+
+        delivered = {0: ()}
+        for sign, at, piece in ring(f_n, part):
+            key = (part, sign, "f", 0, at)
+            dep = () if at == 0 else ((part, sign, "f", 0, at - sign),)
+            send(key, f_name, sign, at, 0, piece, dep)
+            to = (at + sign) % f_n
+            delivered[to] = delivered.get(to, ()) + (key,)
+        for f in sorted(delivered, key=lambda v: min(v, f_n - v)):
+            for sign, at, piece in ring(s_n, 1 if f % 2 == 0 else -1):
+                key = (part, sign, "s", f, at)
+                dep = delivered[f] if at == 0 else ((part, sign, "s", f, at - sign),)
+                send(key, s_name, sign, f, at, piece, dep)
+    for to, keys in blocks.items():
+        out["core", to] = ("c", 1.0, 0.7, tuple(keys), 0)
+        meta["core", to] = ("core", 0, to, 0, 0, Y * CHUNK)
     return out, meta
 
 
 IMAGE_NODES, IMAGE_META = image_nodes()
 IMAGE_EVENTS = order(IMAGE_NODES)
 IMAGE_SLOT = {k: i for i, k in enumerate(IMAGE_META)}
-GRAM_MESSAGES, GRAM_META = gram_messages()
-GRAM_EVENTS = order(GRAM_MESSAGES)
-GRAM_SLOT = {k: i for i, k in enumerate(GRAM_MESSAGES)}
+GRAM_NODES, GRAM_META = gram_nodes()
+GRAM_EVENTS = order(GRAM_NODES)
+GRAM_SLOT = {k: i for i, k in enumerate(GRAM_META)}
 
 
 def combine_kernel(
@@ -194,7 +210,7 @@
     from_z,
     local,
     from_y,
-    total_y,
+    total_x,
     from_x,
     from_line,
     p_send,
@@ -293,10 +309,12 @@
         return remote(src, dst, p_send.at[slot], p_recv.at[slot], peer)
 
     def split(i):
-        count = BLOCK // SPLITS
-        rows = slice(i * count, (i + 1) * count)
-        value = factor_ref[rows, 0, :]
-        high[rows, :], low[rows, :] = halves(value)
+        def some(n, carry):
+            rows = pl.ds(pl.multiple_of(i * (BLOCK // SPLITS) + n * 16, 16), 16)
+            high[rows, :], low[rows, :] = halves(factor_ref[rows, 0, :])
+            return carry
+
+        lax.fori_loop(0, BLOCK // SPLITS // 16, some, 0)
 
     def product(h, far, q):
         side = 1 - hi if far else hi
@@ -361,37 +379,37 @@
         new = image_ref[g, pl.ds(rd * ROWS, ROWS), :]
         local[576 + g : 577 + g, :] = jnp.sum(old * new, axis=0, keepdims=True)
         local[584 + g : 585 + g, :] = jnp.sum(old * old, axis=0, keepdims=True)
-    local[592:640, :] = jnp.zeros((48, 128), jnp.float32)
+    local[592:, :] = jnp.zeros((SLICE - 592, 128), jnp.float32)
+
+    def to_x(d):
+        rows = X_ROWS * wrap(x + d, X)
+        where = pl.ds(pl.multiple_of(rows, 8), X_ROWS)
+        return remote(
+            local.at[where], from_x.at[d - 1], x_send.at[d - 1], x_recv.at[d - 1], x_peer(d)
+        )
+
+    for d in (2, 1, 3):
+        to_x(d).start()
+    for d in range(1, X):
+        to_x(d).wait()
+    strip = local[pl.ds(pl.multiple_of(x * X_ROWS, 8), X_ROWS), :]
+    total_x[...] = (strip + from_x[0]) + (from_x[1] + from_x[2])
 
     def to_y(d):
         where = pl.ds(pl.multiple_of(wrap(y + d, Y) * CHUNK, 8), CHUNK)
         return remote(
-            local.at[where], from_y.at[d - 1], y_send.at[d - 1], y_recv.at[d - 1], y_peer(d)
+            total_x.at[where], from_y.at[d - 1], y_send.at[d - 1], y_recv.at[d - 1], y_peer(d)
         )
 
-    for d in range(1, Y):
+    for d in (4, 3, 5, 2, 6, 1, 7):
         to_y(d).start()
     for d in range(1, Y):
         to_y(d).wait()
-    chunk = local[pl.ds(pl.multiple_of(y * CHUNK, 8), CHUNK), :]
+    chunk = total_x[pl.ds(pl.multiple_of(y * CHUNK, 8), CHUNK), :]
     for d in range(Y - 1):
         chunk = chunk + from_y[d]
-    total_y[...] = chunk
-    from_x[x] = chunk
-
-    def to_x(d, arrived):
-        slot = wrap(x - d, X) if arrived else x
-        return remote(
-            total_y, from_x.at[slot], x_send.at[d - 1], x_recv.at[d - 1], x_peer(d)
-        )
-
-    for d in range(1, X):
-        to_x(d, False).start()
-    for d in range(1, X):
-        to_x(d, True).wait_recv()
-    for d in range(1, X):
-        to_x(d, False).wait_send()
-    from_line[z, hi] = (from_x[0] + from_x[1]) + (from_x[2] + from_x[3])
+
+    from_line[z, hi] = chunk
 
     def to_line(d, e, arrived):
         from_hi = 1 - hi if e and arrived else hi
@@ -402,7 +420,7 @@
     line = [(d, e) for d in (2, 1, 3, 0) for e in (1, 0) if d or e]
     for d, e in line:
         to_line(d, e, False).start()
-    here = pl.ds(pl.multiple_of(y * CHUNK, 8), CHUNK)
+    here = pl.ds(pl.multiple_of((x * Y + y) * CHUNK, 8), CHUNK)
     for d, e in line:
         to_line(d, e, True).wait_recv()
     for d, e in line:
@@ -411,17 +429,19 @@
         parts_ref[k, core, here, :] = (from_line[k, 0] + from_line[k, 1]) * (1.0 / N)
 
     def gram_copy(key, arrived):
-        kind, sign, at, first, count = GRAM_META[key]
+        kind, sign, ox, oy, start, count = GRAM_META[key]
         slot = GRAM_SLOT[key]
-        side = core
-        peer = core_peer
-        if kind == "y":
-            peer = y_peer(sign)
-            at = at + sign if arrived else at
-        elif arrived:
-            side = 1 - core
-        rows = pl.ds(pl.multiple_of(wrap(y - at % Y, Y) * CHUNK, 8), CHUNK)
-        where = parts_ref.at[pl.ds(first, count), side, rows]
+        side, peer = core, core_peer
+        if kind == "core":
+            origin = wrap(x - ox, X) * Y
+            side = 1 - core if arrived else core
+        else:
+            peer = x_peer(sign) if kind == "x" else y_peer(sign)
+            if arrived:
+                ox, oy = (ox + sign, oy) if kind == "x" else (ox, oy + sign)
+            origin = wrap(x - ox % X, X) * Y + wrap(y - oy % Y, Y)
+        rows = pl.ds(pl.multiple_of(origin * CHUNK + start, 8), count)
+        where = parts_ref.at[:, side, rows]
         return remote(where, where, g_send.at[slot], g_recv.at[slot], peer)
 
     for event, key in GRAM_EVENTS:
@@ -429,7 +449,7 @@
             gram_copy(key, False).start()
         else:
             gram_copy(key, True).wait_recv()
-    for key in GRAM_MESSAGES:
+    for key in GRAM_META:
         gram_copy(key, False).wait_send()
 
 
@@ -457,14 +477,14 @@
             pltpu.VMEM((2, Z - 1, BLOCK // 2, 128), f32),
             pltpu.VMEM((SLICE, 128), f32),
             pltpu.VMEM((Y - 1, CHUNK, 128), f32),
-            pltpu.VMEM((CHUNK, 128), f32),
-            pltpu.VMEM((X, CHUNK, 128), f32),
+            pltpu.VMEM((X_ROWS, 128), f32),
+            pltpu.VMEM((X - 1, X_ROWS, 128), f32),
             pltpu.VMEM((Z, 2, CHUNK, 128), f32),
             *pair(len(IMAGE_META)),
             *pair(Y - 1),
             *pair(X - 1),
             *pair(2 * Z),
-            *pair(len(GRAM_MESSAGES)),
+            *pair(len(GRAM_META)),
         ],
         compiler_params=pltpu.CompilerParams(
             collective_id=0, has_side_effects=True, vmem_limit_bytes=50 << 20

time: 199 us -> 197 us (0.990)
  Pallas kernels: 197 us -> 192 us
  local copies, waits for them, and re-layouts: 1.01 us -> 4.64 us
    pallas_call x1, Pallas kernels: 155 us -> 150 us  [combine(): pl.pallas_call(combine_kernel, out_shape=(jax.ShapeDtypeStruct((8, BLOCK,...]
    unnamed x0 -> x4, local copies, waits for them, and re-layouts: none -> 3.63 us
where the time goes in v4:
time: 197 us
  Pallas kernels  192 us (97%)
  local copies, waits for them, and re-layouts  4.64 us (2%)
    pallas_call x1, Pallas kernels, combine(): pl.pallas_call(combine_kernel, out_shape=(jax.ShapeDtypeStruct((8, BLOCK,...  150 us
    pallas_call x1, Pallas kernels, refresh(): pl.pallas_call(refresh_kernel, out_shape=(jax.ShapeDtypeStruct((BLOCK, 10...  42.1 us

profile of v4, /device:TPU:1, one launch (start us, length us, event | category | flops | bytes accessed | tf_op | source)
XLA Modules:
  0.0 197.2 jit_solution(8956380731821531740)
XLA Ops:
  0.6 1.0 reshape.19
  1.7 0.0 copy-start
  1.7 1.7 copy-done
  3.4 149.8 %combine.1 = (f32[8,288,128]{2,1,0:T(8,128)S(1)}, f32[4,2,768,128]{3,2,1,0:T(8,128)}) custom-call(f32[288,1,2304]{2,1,0:T(1,128)S(1)} %copy-done, f32[2,144,128]{2,1,0:T(8,128)S(1)} %bitcast.6), custom_call_target="tpu_custom_call" | custom-call | flops 5000000000 | bytes 8388608 | tf_op jit(solution)/shard_map/combine/pallas_call | solution.py:463
  153.2 0.0 copy-start.1
  153.2 1.9 copy-done.1
  155.1 42.1 %refresh.1 = (f32[288,1024]{1,0:T(8,128)}, f32[8,128]{1,0:T(8,128)}) custom-call(f32[6144,128]{1,0:T(8,128)S(1)} %bitcast.7, f32[2304,128]{1,0:T(8,128)S(1)} %bitcast.8), custom_call_target="tpu_custom_call" | custom-call | flops 3000000000 | bytes 5242880 | tf_op jit(solution)/shard_map/refresh/pallas_call | solution.py:614
  (1 shorter events, 0.0 us)
Async XLA Ops:
  1.7 1.8 copy-start
  153.2 1.9 copy-start.1

commit v5 on v4

--- a/solution.py
+++ b/solution.py
@@ -89,14 +89,14 @@
     splits = tuple(("split", i) for i in range(SPLITS))
     products = {0: [], 1: []}
     early = []
-    for unit, (h, far) in enumerate(((0, 0), (0, 1), (1, 2))):
+    for unit, (h, far) in enumerate(((0, 0), (0, 1), (1, 0), (1, 1))):
         needs = ()
         if far:
             z_key = ("hi", h)
-            out[z_key] = ("z", HALF * 1024 / 50e3, 3.0, (), h)
+            before = (("hi", 0),) if h else ()
+            out[z_key] = ("z", 6.0, 4.0, before, h)
             meta[z_key] = ("hi", h, 0, 0, 0, 0, 0, HALF)
             needs = (z_key,)
-        wide = 2 if far == 2 else 1
         arrivals = []
         for part, (first, rows) in enumerate(((0, 22), (22, 14))):
             axes = (("y", Y), ("x", X)) if part == 0 else (("x", X), ("y", Y))
@@ -111,7 +111,7 @@
             def send(key, name, sign, f, s, piece, dep):
                 start, count = cut(piece)
                 ox, oy = (f, s) if f_name == "x" else (s, f)
-                took = count * 4 * 512 * wide / rate
+                took = count * 4 * 512 / rate
                 out[key] = (name + str(sign), took, 1.0, dep, 2 * unit + (key[3] != "f"))
                 meta[key] = (name, h, far, sign, ox, oy, start * 4, count * 4)
                 arrivals.append(key)
@@ -132,11 +132,11 @@
                     send(key, s_name, sign, f, at, piece, dep)
         if unit == 0:
             early = arrivals
-        for side in (far,) if far < 2 else (0, 1):
-            for q in range(2):
-                key = ("product", h, side, q)
-                out[key] = ("tc", 0.8, 0.0, needs + tuple(arrivals) + splits, 0)
-                products[h].append(key)
+        for q in range(2):
+            key = ("product", h, far, q)
+            last = (("product", h, 0, q),) if far else ()
+            out[key] = ("tc", 0.8, 0.0, needs + tuple(arrivals) + splits + last, 0)
+            products[h].append(key)
     for i, key in enumerate(splits):
         out[key] = ("tc", 0.5, 0.0, (early[4 + 6 * i],), 1)
     for h in range(2):
@@ -198,10 +198,12 @@
 
 
 def combine_kernel(
-    factor_ref,
+    factor_hbm,
     panel_ref,
     image_ref,
     parts_ref,
+    factor_ref,
+    factor_sem,
     gathered,
     high,
     low,
@@ -260,6 +262,8 @@
             device_id_type=MESH,
         )
 
+    load = pltpu.make_async_copy(factor_hbm, factor_ref, factor_sem)
+    load.start()
     barrier = pltpu.get_barrier_semaphore()
     peers = [x_peer(d) for d in range(1, X)] + [y_peer(d) for d in range(1, Y)]
     peers += [line_peer(d, e) for e in range(2) for d in range(1 - e, Z)] + [core_peer]
@@ -283,7 +287,7 @@
                 side = 1 - hi if arrived else hi
             else:
                 peer = x_peer(sign) if kind == "x" else y_peer(sign)
-                side = (hi, 1 - hi, slice(None))[far]
+                side = 1 - hi if far else hi
                 if arrived:
                     ox, oy = (ox + sign, oy) if kind == "x" else (ox, oy + sign)
             origin = wrap(x - ox % X, X) * Y + wrap(y - oy % Y, Y)
@@ -309,6 +313,9 @@
         return remote(src, dst, p_send.at[slot], p_recv.at[slot], peer)
 
     def split(i):
+        if i == 0:
+            load.wait()
+
         def some(n, carry):
             rows = pl.ds(pl.multiple_of(i * (BLOCK // SPLITS) + n * 16, 16), 16)
             high[rows, :], low[rows, :] = halves(factor_ref[rows, 0, :])
@@ -466,9 +473,11 @@
             jax.ShapeDtypeStruct((8, BLOCK, 128), f32),
             jax.ShapeDtypeStruct((Z, 2, SLICE, 128), f32),
         ),
-        in_specs=[vmem, vmem],
+        in_specs=[pl.BlockSpec(memory_space=pl.ANY), vmem],
         out_specs=(vmem, vmem),
         scratch_shapes=[
+            pltpu.VMEM((BLOCK, 1, 8 * BLOCK), f32),
+            pltpu.SemaphoreType.DMA(()),
             pltpu.VMEM((2, 2, SIDE, 128), f32),
             pltpu.VMEM((BLOCK, 8 * BLOCK), bf16),
             pltpu.VMEM((BLOCK, 8 * BLOCK), bf16),
@@ -487,7 +496,7 @@
             *pair(len(GRAM_META)),
         ],
         compiler_params=pltpu.CompilerParams(
-            collective_id=0, has_side_effects=True, vmem_limit_bytes=50 << 20
+            collective_id=0, has_side_effects=True, vmem_limit_bytes=58 << 20
         ),
         cost_estimate=pl.CostEstimate(
             flops=5 * 10**9, bytes_accessed=8 << 20, transcendentals=0

time: 197 us -> 202 us (1.025)
  Pallas kernels: 192 us -> 196 us
    pallas_call x1, Pallas kernels: 150 us -> 154 us  [combine(): pl.pallas_call(combine_kernel, out_shape=(jax.ShapeDtypeStruct((8, BLOCK,...]
where the time goes in v5:
time: 202 us
  Pallas kernels  196 us (97%)
  local copies, waits for them, and re-layouts  4.83 us (2%)
    pallas_call x1, Pallas kernels, combine(): pl.pallas_call(combine_kernel, out_shape=(jax.ShapeDtypeStruct((8, BLOCK,...  154 us
    pallas_call x1, Pallas kernels, refresh(): pl.pallas_call(refresh_kernel, out_shape=(jax.ShapeDtypeStruct((BLOCK, 10...  42.1 us

profile of v5, /device:TPU:1, one launch (start us, length us, event | category | flops | bytes accessed | tf_op | source)
XLA Modules:
  0.0 201.9 jit_solution(17300198972857520006)
XLA Ops:
  0.6 1.0 reshape.19
  1.6 0.7 copy.4
  2.3 154.3 %combine.1 = (f32[8,288,128]{2,1,0:T(8,128)}, f32[4,2,768,128]{3,2,1,0:T(8,128)}) custom-call(f32[288,1,2304]{2,1,0:T(1,128)} %factor_hbm.1, f32[2,144,128]{2,1,0:T(8,128)} %bitcast.8), custom_call_target="tpu_custom_call" | custom-call | flops 5000000000 | bytes 8388608 | tf_op jit(solution)/shard_map/combine/pallas_call | solution.py:470
  156.6 0.0 copy-start
  156.6 1.9 copy-done
  158.5 0.0 copy-start.1
  158.5 1.3 copy-done.1
  159.7 42.1 %refresh.1 = (f32[288,1024]{1,0:T(8,128)}, f32[8,128]{1,0:T(8,128)}) custom-call(f32[6144,128]{1,0:T(8,128)S(1)} %bitcast.6, f32[2304,128]{1,0:T(8,128)S(1)} %bitcast.7), custom_call_target="tpu_custom_call" | custom-call | flops 3000000000 | bytes 5242880 | tf_op jit(solution)/shard_map/refresh/pallas_call | solution.py:623
Async XLA Ops:
  156.6 1.9 copy-start
  158.5 1.3 copy-start.1
